TPU v7x, 512 devices: a whole 4x8x8 slice. The times are simulated.
512 devices in a mesh: dp: 2 (over y_lo), cand: 32 (over z, y_hi), tensor: 8 (over x, core).
Axes of the slice: x: 4, y: 8 (y_hi: 4, y_lo: 2; y = y_hi * 2 + y_lo), z: 8, core: 2. Of those that a mesh axis runs over, the one named last changes fastest.
Arguments:
- cand_query: bfloat16 [2, 64, 128, 4096], P('dp', 'cand', None, 'tensor'), may hold values from -88 to 88
- cand_key: bfloat16 [2, 64, 128, 1024], P('dp', 'cand', None, 'tensor'), may hold values from -4 to 4
- shared_prefix_key: bfloat16 [2, 1024, 1024], P('dp', 'cand', 'tensor'), may hold values from -4 to 4
- cand_hidden: bfloat16 [2, 64, 128, 4096], P('dp', 'cand', 'tensor'), may hold values from -6 to 6
- prefix_hidden: bfloat16 [2, 1024, 4096], P('dp', ('cand', 'tensor')), may hold values from -6 to 6
- value_matrix: bfloat16 [4096, 1024], P(None, 'tensor'), may hold values from -0.09375 to 0.09375
- out_cotangent: bfloat16 [2, 64, 128, 4096], P('dp', 'cand', None, 'tensor'), may hold values from -96 to 96
- cand_scores: float32 [2, 64], P('dp', 'cand'), may hold values from -15 to 315
- ranking: int32 [2, 64], P('dp'), may hold values from 0 to 63, each once within a row
- lengths: int32 [2, 64], P('dp', 'cand'), may hold values from 2 to 128, as said below
Outputs:
- grad_query: bfloat16 [2, 64, 128, 4096], P('dp', 'cand', None, 'tensor')
- grad_cand_key: bfloat16 [2, 64, 128, 1024], P('dp', 'cand', None, 'tensor')
- grad_prefix_key: bfloat16 [2, 1024, 1024], P('dp', 'cand', 'tensor')
- grad_prefix_value: bfloat16 [2, 1024, 1024], P('dp', 'cand', 'tensor')
- grad_value_weight: float32 [4096, 1024], P(('dp', 'cand'), 'tensor')
Inputs may be any that keep to these rules, and one draw needn't show every extreme that they name: `lengths`: every list has a candidate of exactly 128 tokens.
All inputs are finite; a program needn't handle non-finite values.
Results may differ from a plain program's by a relative error of at most 0.012.
Values may be sent and summed in bfloat16 or wider, within the bound.
A program may use at most 64 MiB of HBM per device.

v0:
```python
import jax
import jax.numpy as jnp
from jax import lax
from jax.experimental import pallas as pl
from jax.experimental.pallas import tpu as pltpu
from jax.sharding import PartitionSpec as P

MESH = pl.DeviceIdType.MESH
BF16, F32 = jnp.bfloat16, jnp.float32
NZ, NYH, NY, NX, NT = 8, 4, 8, 4, 8
HEAD = 128
PREFIX = 1024
CAND = 128
CHUNK = 256
WIDTH = 4096
INV_ROOT = HEAD ** (-0.5)


def dot(a, b):
    return lax.dot_general(a, b, (((1,), (0,)), ((), ())), preferred_element_type=F32)


def dot_nt(a, b):
    return lax.dot_general(a, b, (((1,), (1,)), ((), ())), preferred_element_type=F32)


class Exchange:
    def __init__(self, n, me, device, src, dst, sems):
        self.n, self.me, self.device, self.src, self.dst, self.sems = n, me, device, src, dst, sems

    def copy(self, k, slot):
        peer = lax.rem(self.me + k, self.n)
        return pltpu.make_async_remote_copy(
            src_ref=self.src(peer),
            dst_ref=self.dst(slot),
            send_sem=self.sems.at[0, k],
            recv_sem=self.sems.at[1, k],
            device_id=self.device(peer),
            device_id_type=MESH,
        )

    def loop(self, step):
        def body(k, carry):
            step(k)
            return carry

        lax.fori_loop(1, self.n, body, 0)

    def start(self):
        self.loop(lambda k: self.copy(k, self.me).start())

    def wait_recv(self):
        self.loop(lambda k: self.copy(k, lax.rem(self.me + self.n - k, self.n)).wait_recv())

    def wait_send(self):
        self.loop(lambda k: self.copy(k, self.me).wait_send())


class Ring:
    def __init__(self, me, device, whole, half, third, fourth, joined, came, sems):
        self.me, self.device, self.whole, self.half = me, device, whole, half
        self.third, self.fourth, self.joined, self.came = third, fourth, joined, came

        def copy(i, src, dst, offset):
            return pltpu.make_async_remote_copy(
                src_ref=src,
                dst_ref=dst,
                send_sem=sems.at[0, i],
                recv_sem=sems.at[1, i],
                device_id=device(lax.rem(me + offset + 8, 8)),
                device_id_type=MESH,
            )

        self.first = (
            copy(0, self.block(3), third.at[0], 1),
            copy(1, self.block(-3), third.at[1], -1),
            copy(2, self.block(4, 0, 4), fourth.at[0], 2),
            copy(3, self.block(4, 4, 4), fourth.at[1], -2),
        )
        self.near = (
            copy(4, self.block(1), came.at[0], 1),
            copy(5, self.block(-1), came.at[1], -1),
        )
        self.second = (
            copy(6, joined.at[0], came.at[2], 2),
            copy(7, joined.at[1], came.at[3], -2),
        )

    def block(self, offset, start=0, count=8):
        slot = lax.rem(self.me + offset + 8, 8) * 8 + start
        return self.whole.at[self.half, pl.ds(slot, count)]

    def start(self):
        for one in self.first + self.near:
            one.start()

    def relay(self):
        for one in self.first:
            one.wait_recv()
        for side, offset in ((0, 2), (1, -2)):
            own = self.block(offset)[...].astype(F32) + self.third[side].astype(F32)
            part = slice(side * 4, side * 4 + 4)
            rest = slice(4 - side * 4, 8 - side * 4)
            self.joined[side, part] = (own[part] + self.fourth[side].astype(F32)).astype(BF16)
            self.joined[side, rest] = own[rest].astype(BF16)
            self.second[side].start()

    def total(self):
        result = self.block(0)[...].astype(F32)
        for i, one in enumerate(self.near + self.second):
            one.wait_recv()
            result = result + self.came[i].astype(F32)
        return result

    def wait_send(self):
        for one in self.first + self.near + self.second:
            one.wait_send()


def rank_gradient(scores_row, ranking_row):
    n = ranking_row.shape[1]
    rows = lax.broadcasted_iota(jnp.int32, (n, n), 0)
    cols = lax.broadcasted_iota(jnp.int32, (n, n), 1)
    scores_col = jnp.sum(jnp.where(rows == cols, scores_row, 0.0), axis=1, keepdims=True)
    picker = ranking_row == rows
    ordered = jnp.sum(jnp.where(picker, scores_col, 0.0), axis=0, keepdims=True)
    later = cols >= rows
    masked = jnp.where(later, ordered, -jnp.inf)
    top = jnp.max(masked, axis=1, keepdims=True)
    weights = jnp.exp(masked - top)
    suffix = weights / jnp.sum(weights, axis=1, keepdims=True)
    by_rank = jnp.sum(suffix, axis=0, keepdims=True) - 1.0
    return jnp.sum(jnp.where(picker, by_rank, 0.0), axis=1, keepdims=True)


def kernel(
    q_hbm, ck_hbm, pk_hbm, ch_hbm, ph_hbm, w_hbm, oc_hbm, sc_ref, rk_ref, ln_ref,
    gq_hbm, gck_hbm, gpk_hbm, gpv_hbm, gw_hbm,
    gq_ref, gck_ref, gpk_ref, gpv_ref, gw_ref, store_sem,
    q_ref, ck_ref, pk_ref, ph_ref, w_ref, oc_ref, load_sem,
    phs_ref, own_hp, sxa, sxb, xa, xb, ga, gb,
    hc_ref, hp_ref, kall_ref, vall_ref, kt_ref, s1_ref, s2_ref,
    qs_ref, cs_ref, p_ref, vc_ref, dvp_ref, dvc_ref, dkp_ref, dkc_ref, dvr_ref,
    send_v, send_k, rva1, rvb1, rva2, rvb2, rka1, rkb1, rka2, rkb2, tva2, tvb2, tka2, tkb2,
    send_w, third_a, fourth_a, joined_a, came_a, third_b, fourth_b, joined_b, came_b,
    rwa2, rwb2, twa2, twb2,
    sem_hp, sem_hx, sem_hs, sem_s, sem_k, sem_v, sem_dv, sem_dk, sem_dw, sem_r, sem_x, sem_g,
):
    dp = lax.axis_index("dp")
    cand = lax.axis_index("cand")
    tens = lax.axis_index("tensor")
    z, yh = cand // NYH, lax.rem(cand, NYH)
    y = yh * 2 + dp
    x, core = tens // 2, lax.rem(tens, 2)
    other = 1 - core

    def at_t(t):
        return (dp, cand, t)

    def at_x(xx):
        return (dp, cand, xx * 2 + core)

    def at_z(zz):
        return (dp, zz * NYH + yh, tens)

    def at_yh(yy):
        return (dp, z * NYH + yy, tens)

    def at_y(yy):
        return (lax.rem(yy, 2), z * NYH + yy // 2, tens)

    barrier = pltpu.get_barrier_semaphore()
    for n, me, device in ((NT, tens, at_t), (NZ, z, at_z), (NY, y, at_y)):
        def greet(k, carry, n=n, me=me, device=device):
            pl.semaphore_signal(
                barrier, inc=1, device_id=device(lax.rem(me + k, n)), device_id_type=MESH
            )
            return carry

        lax.fori_loop(1, n, greet, 0)

    loads = [
        pltpu.make_async_copy(src, dst, load_sem.at[i])
        for i, (src, dst) in enumerate((
            (pk_hbm, pk_ref), (ph_hbm, ph_ref), (ch_hbm, hc_ref.at[tens]), (q_hbm, q_ref),
            (ck_hbm, ck_ref), (w_hbm, w_ref), (oc_hbm, oc_ref),
        ))
    ]
    for load in loads:
        load.start()
    stores = [
        pltpu.make_async_copy(src, dst, store_sem.at[i])
        for i, (src, dst) in enumerate((
            (gq_ref, gq_hbm), (gck_ref, gck_hbm), (gpk_ref, gpk_hbm), (gpv_ref, gpv_hbm),
            (gw_ref, gw_hbm),
        ))
    ]

    loads[0].wait()
    kall_ref[0, z * NYH + yh] = pk_ref[0]
    kall_ref[1, yh * NZ + z] = pk_ref[1]
    loads[1].wait()
    own_rows = ph_ref[...].astype(F32)
    for b in range(4):
        phs_ref[b * 4:(b + 1) * 4, :] = own_rows[:, b * 1024:(b + 1) * 1024]
    own_hp[...] = phs_ref[...].astype(BF16)
    hp_ref[tens] = own_hp[...]
    loads[2].wait()
    loads[3].wait()
    lane = lax.broadcasted_iota(jnp.int32, (8, 128), 1)
    own_scores = jnp.where(
        lane == 2 * cand, sc_ref[0, 0], jnp.where(lane == 2 * cand + 1, sc_ref[0, 1], 0.0)
    )
    s1_ref[yh] = own_scores
    for c in range(2):
        for r in range(4):
            base = c * 512 + r * 128
            qs_ref[base:base + 128, :] = q_ref[c, :, r * 128:(r + 1) * 128]
    dvp_ref[...] = jnp.zeros_like(dvp_ref)
    dvc_ref[...] = jnp.zeros_like(dvc_ref)
    dkp_ref[...] = jnp.zeros_like(dkp_ref)
    dkc_ref[...] = jnp.zeros_like(dkc_ref)
    for load in loads[4:]:
        load.wait()

    pl.semaphore_wait(barrier, (NT - 1) + (NZ - 1) + (NY - 1))

    def gather(own, whole, sems):
        a1 = Exchange(NYH, yh, at_yh, lambda p: own.at[0],
                      lambda s: whole.at[0, z * NYH + s], sems.at[0])
        b1 = Exchange(NZ, z, at_z, lambda p: own.at[1],
                      lambda s: whole.at[1, yh * NZ + s], sems.at[1])
        a2 = Exchange(NZ, z, at_z, lambda p: whole.at[0, pl.ds(z * NYH, NYH)],
                      lambda s: whole.at[0, pl.ds(s * NYH, NYH)], sems.at[2])
        b2 = Exchange(NYH, yh, at_yh, lambda p: whole.at[1, pl.ds(yh * NZ, NZ)],
                      lambda s: whole.at[1, pl.ds(s * NZ, NZ)], sems.at[3])
        return a1, b1, a2, b2

    hp_x = Exchange(NT, tens, at_t, lambda p: own_hp, lambda s: hp_ref.at[s], sem_hp)
    hc_x = Exchange(NX, x, at_x, lambda p: hc_ref.at[tens],
                    lambda s: hc_ref.at[s * 2 + core], sem_hx)
    s_1 = Exchange(NYH, yh, at_yh, lambda p: s1_ref.at[yh], lambda s: s1_ref.at[s], sem_s.at[0])
    s_2 = Exchange(NZ, z, at_z, lambda p: s2_ref.at[z], lambda s: s2_ref.at[s], sem_s.at[1])
    k_a1, k_b1, k_a2, k_b2 = gather(pk_ref, kall_ref, sem_k)

    def sibling(xx, mine):
        slot = xx * 2 + (core if mine else other)
        return pltpu.make_async_remote_copy(
            src_ref=hc_ref.at[xx * 2 + core],
            dst_ref=hc_ref.at[slot],
            send_sem=sem_hs.at[0, xx],
            recv_sem=sem_hs.at[1, xx],
            device_id=(dp, cand, x * 2 + other),
            device_id_type=MESH,
        )

    k_a1.start()
    k_b1.start()
    s_1.start()
    hp_x.start()
    hc_x.start()
    sibling(x, True).start()

    k_a1.wait_recv()
    k_a2.start()
    k_b1.wait_recv()
    k_b2.start()
    s_1.wait_recv()
    s2_ref[z] = s1_ref[0] + s1_ref[1] + s1_ref[2] + s1_ref[3]
    s_2.start()

    hp_x.wait_recv()
    to = lax.broadcasted_iota(jnp.int32, (128, 128), 0)
    came = lax.broadcasted_iota(jnp.int32, (128, 128), 1)
    order = came == lax.rem(to // 4, 8) * 16 + (to // 32) * 4 + lax.rem(to, 4)
    hp_rows = dot(
        jnp.where(order, 1.0, 0.0).astype(BF16), hp_ref[...].reshape(128, 1024)
    ).astype(BF16)
    pv = jnp.zeros((32, HEAD), F32)
    for b in range(4):
        pv = pv + dot(hp_rows[b * 32:(b + 1) * 32], w_ref[b * 1024:(b + 1) * 1024, :])
    pv = pv.astype(BF16).reshape(2, 16, HEAD)
    vall_ref[0, z * NYH + yh] = pv[0]
    vall_ref[1, yh * NZ + z] = pv[1]

    class Own:
        def __init__(self, first, second):
            self.at = (first, second)

    v_a1, v_b1, v_a2, v_b2 = gather(
        Own(vall_ref.at[0, z * NYH + yh], vall_ref.at[1, yh * NZ + z]), vall_ref, sem_v
    )
    v_a1.start()
    v_b1.start()

    spot = lax.broadcasted_iota(jnp.int32, (1, 1024), 1)
    place = lax.rem(spot, 512)
    outer, inner, last = place // 128, lax.rem(place // 32, 4), lax.rem(spot, 32)
    wanted = jnp.where(
        spot < 512, outer * 256 + inner * 64 + last, inner * 256 + outer * 64 + 32 + last
    )
    sorted_hp = jnp.zeros((128, 1024), F32)
    for b in range(4):
        row = lax.broadcasted_iota(jnp.int32, (256, 1024), 0) + b * 256
        pick = jnp.where(row == wanted, 1.0, 0.0).astype(BF16)
        sorted_hp = sorted_hp + dot(hp_rows[:, b * 256:(b + 1) * 256], pick)
    sorted_hp = sorted_hp.astype(BF16)
    for d in range(2):
        for zh in range(2):
            rows = sorted_hp[(d * 2 + zh) * 32:(d * 2 + zh + 1) * 32]
            for j in range(4):
                sxa[zh * 4 + j, :, d * 128:(d + 1) * 128] = rows[:, j * 128:(j + 1) * 128]
                sxb[j * 2 + d, :, zh * 128:(zh + 1) * 128] = (
                    rows[:, 512 + j * 128:512 + (j + 1) * 128]
                )
    xa[z] = sxa[z]
    xb[y] = sxb[y]
    x_a = Exchange(NZ, z, at_z, lambda p: sxa.at[p], lambda s: xa.at[s], sem_x.at[0])
    x_b = Exchange(NY, y, at_y, lambda p: sxb.at[p], lambda s: xb.at[s], sem_x.at[1])
    x_a.start()
    x_b.start()

    s_2.wait_recv()
    total = s2_ref[0]
    for i in range(1, NZ):
        total = total + s2_ref[i]
    list_grad = rank_gradient(total[0:1, 0:64], rk_ref[...])
    item = lax.broadcasted_iota(jnp.int32, (64, 1), 0)
    for c in range(2):
        own_grad = jnp.sum(
            jnp.where(item == 2 * cand + c, list_grad, 0.0), axis=0, keepdims=True
        )
        live = lax.broadcasted_iota(jnp.int32, (CAND, 128), 0) < ln_ref[0, c]
        for r in range(4):
            base = c * 512 + r * 128
            part = oc_ref[c, :, r * 128:(r + 1) * 128].astype(F32) * own_grad
            cs_ref[base:base + 128, :] = jnp.where(live, part, 0.0).astype(BF16)

    k_a2.wait_recv()
    k_b2.wait_recv()
    kt_ref[...] = kall_ref[...].reshape(PREFIX, HEAD).astype(F32).T.astype(BF16)

    def soft(n, carry):
        c = n // 2
        cols = pl.ds(pl.multiple_of(n * CHUNK, CHUNK), CHUNK)
        queries = qs_ref[cols, :]
        cot = cs_ref[cols, :]
        log_p = dot_nt(kall_ref[...].reshape(PREFIX, HEAD), queries) * INV_ROOT
        log_c = dot_nt(ck_ref[c], queries) * INV_ROOT
        slot = lax.broadcasted_iota(jnp.int32, (CAND, CHUNK), 0)
        position = lax.rem(lax.broadcasted_iota(jnp.int32, (CAND, CHUNK), 1), CAND)
        allowed = (slot <= position) & (slot < ln_ref[0, c])
        log_c = jnp.where(allowed, log_c, -jnp.inf)
        top = jnp.maximum(
            jnp.max(log_p, axis=0, keepdims=True), jnp.max(log_c, axis=0, keepdims=True)
        )
        exp_p = jnp.exp(log_p - top)
        exp_c = jnp.exp(log_c - top)
        inverse = 1.0 / (
            jnp.sum(exp_p, axis=0, keepdims=True) + jnp.sum(exp_c, axis=0, keepdims=True)
        )
        prob_p = exp_p * inverse
        prob_c = exp_c * inverse
        p_ref[0:PREFIX, cols] = prob_p
        p_ref[PREFIX:PREFIX + CAND, cols] = prob_c
        dvp_ref[...] += dot(prob_p.astype(BF16), cot)
        dvc_ref[c] += dot(prob_c.astype(BF16), cot)
        return carry

    def pass_on(k, carry):
        sender = lax.rem(x + NX - k, NX)
        hc_x.copy(k, sender).wait_recv()
        sibling(sender, True).start()
        return carry

    lax.fori_loop(0, 1, soft, 0)
    v_a1.wait_recv()
    v_a2.start()
    v_b1.wait_recv()
    v_b2.start()
    lax.fori_loop(1, 3, soft, 0)
    lax.fori_loop(1, NX, pass_on, 0)
    lax.fori_loop(3, 4, soft, 0)

    def scatter(whole, ra1, rb1, ra2, rb2, ta2, tb2, sems, ny, my_y, at_group):
        a1 = Exchange(NZ, z, at_z, lambda p: whole.at[0, pl.ds(p * ny, ny)],
                      lambda s: ra1.at[s], sems.at[0])
        b1 = Exchange(ny, my_y, at_group, lambda p: whole.at[1, pl.ds(p * NZ, NZ)],
                      lambda s: rb1.at[s], sems.at[1])
        a2 = Exchange(ny, my_y, at_group, lambda p: ta2.at[p], lambda s: ra2.at[s], sems.at[2])
        b2 = Exchange(NZ, z, at_z, lambda p: tb2.at[p], lambda s: rb2.at[s], sems.at[3])

        def middle():
            a1.wait_recv()
            ra1[z] = whole[0, pl.ds(z * ny, ny)]
            total = ra1[0].astype(F32)
            for i in range(1, NZ):
                total = total + ra1[i].astype(F32)
            ta2[...] = total.astype(BF16)
            a2.start()
            b1.wait_recv()
            rb1[my_y] = whole[1, pl.ds(my_y * NZ, NZ)]
            total = rb1[0].astype(F32)
            for i in range(1, ny):
                total = total + rb1[i].astype(F32)
            tb2[...] = total.astype(BF16)
            b2.start()

        def end():
            a2.wait_recv()
            ra2[my_y] = ta2[my_y]
            first = ra2[0].astype(F32)
            for i in range(1, ny):
                first = first + ra2[i].astype(F32)
            b2.wait_recv()
            rb2[z] = tb2[z]
            second = rb2[0].astype(F32)
            for i in range(1, NZ):
                second = second + rb2[i].astype(F32)
            return first, second

        return (a1, b1, a2, b2), middle, end

    dv_all, dv_middle, dv_end = scatter(
        send_v, rva1, rvb1, rva2, rvb2, tva2, tvb2, sem_dv, NYH, yh, at_yh
    )
    send_v[...] = dvp_ref[...].astype(BF16).reshape(2, 32, 16, HEAD)
    dv_all[0].start()
    dv_all[1].start()

    def from_sibling(k, carry):
        sibling(k, False).wait_recv()
        return carry

    lax.fori_loop(0, NX, from_sibling, 0)
    for c in range(2):
        dvr_ref[:, c] = dvc_ref[c].reshape(8, 16, HEAD)
    dvr_t = dvr_ref[...].reshape(256, HEAD).T.astype(BF16)

    def weight(b, carry):
        cols = pl.ds(pl.multiple_of(b * 512, 512), 512)
        part = dot(dvr_t, hc_ref[:, :, cols].reshape(256, 512))
        rows = part.T.astype(BF16).reshape(2, NYH, 2, 32, HEAD)
        d, zz = b // 4, lax.rem(b, 4) * 2
        for i in range(2):
            for j in range(NYH):
                send_w[0, (zz + i) * NY + j * 2 + d] = rows[i, j, 0]
                send_w[1, (j * 2 + d) * NZ + zz + i] = rows[i, j, 1]
        return carry

    lax.fori_loop(0, 8, weight, 0)
    ring_a = Ring(z, at_z, send_w, 0, third_a, fourth_a, joined_a, came_a, sem_r.at[0])
    ring_b = Ring(y, at_y, send_w, 1, third_b, fourth_b, joined_b, came_b, sem_r.at[1])
    dw_a = Exchange(NY, y, at_y, lambda p: twa2.at[p], lambda s: rwa2.at[s], sem_dw.at[0])
    dw_b = Exchange(NZ, z, at_z, lambda p: twb2.at[p], lambda s: rwb2.at[s], sem_dw.at[1])
    dv_middle()
    ring_a.start()
    ring_b.start()

    cv = dot(hc_ref[...].reshape(256, WIDTH), w_ref[...]).astype(BF16).reshape(8, 2, 16, HEAD)
    for c in range(2):
        vc_ref[c] = cv[:, c].reshape(CAND, HEAD)
    v_a2.wait_recv()
    v_b2.wait_recv()

    def score(n, carry):
        c = n // 2
        cols = pl.ds(pl.multiple_of(n * CHUNK, CHUNK), CHUNK)
        queries = qs_ref[cols, :]
        cot = cs_ref[cols, :]
        dprob_p = dot_nt(vall_ref[...].reshape(PREFIX, HEAD), cot)
        dprob_c = dot_nt(vc_ref[c], cot)
        prob_p = p_ref[0:PREFIX, cols]
        prob_c = p_ref[PREFIX:PREFIX + CAND, cols]
        row_total = jnp.sum(prob_p * dprob_p, axis=0, keepdims=True) + jnp.sum(
            prob_c * dprob_c, axis=0, keepdims=True
        )
        ds_p = (prob_p * (dprob_p - row_total)).astype(BF16)
        ds_c = (prob_c * (dprob_c - row_total)).astype(BF16)
        dkp_ref[...] += dot(ds_p, queries)
        dkc_ref[c] += dot(ds_c, queries)
        kc_t = ck_ref[c].astype(F32).T.astype(BF16)
        gq_t = (dot(kt_ref[...], ds_p) + dot(kc_t, ds_c)) * INV_ROOT
        p_ref[0:128, cols] = gq_t
        return carry

    lax.fori_loop(0, 1, score, 0)
    ring_a.relay()
    ring_b.relay()
    lax.fori_loop(1, 2, score, 0)

    first, second = dv_end()
    gpv_ref[0] = first.astype(BF16)
    gpv_ref[1] = second.astype(BF16)
    stores[3].start()
    ga[z] = gpv_ref[...]
    gb[y] = gpv_ref[...]
    g_a = Exchange(NZ, z, at_z, lambda p: ga.at[z], lambda s: ga.at[s], sem_g.at[0])
    g_b = Exchange(NY, y, at_y, lambda p: gb.at[y], lambda s: gb.at[s], sem_g.at[1])
    g_a.start()
    g_b.start()
    lax.fori_loop(2, 4, score, 0)

    dk_all, dk_middle, dk_end = scatter(
        send_k, rka1, rkb1, rka2, rkb2, tka2, tkb2, sem_dk, NYH, yh, at_yh
    )
    send_k[...] = (dkp_ref[...] * INV_ROOT).astype(BF16).reshape(2, 32, 16, HEAD)
    dk_all[0].start()
    dk_all[1].start()

    for c in range(2):
        gck_ref[c] = (dkc_ref[c] * INV_ROOT).astype(BF16)
        for r in range(4):
            base = c * 512 + r * 128
            gq_ref[c, :, r * 128:(r + 1) * 128] = (
                p_ref[0:128, base:base + 128].T.astype(BF16)
            )
    stores[0].start()
    stores[1].start()

    x_a.wait_recv()
    x_b.wait_recv()

    def prefix_part(half):
        (g_a, g_b)[half].wait_recv()
        rows = (ga, gb)[half][...].reshape(256, HEAD).astype(F32).T.astype(BF16)
        part = dot(rows, (xa, xb)[half][...].reshape(256, 256))
        part = part.T
        if half == 0:
            part = part.reshape(2, NYH, 32, HEAD).swapaxes(0, 1)
        return part.reshape(8, 32, HEAD)

    twa2[...] = (ring_a.total() + prefix_part(0)).astype(BF16)
    dw_a.start()
    twb2[...] = (ring_b.total() + prefix_part(1)).astype(BF16)
    dw_b.start()
    dk_middle()
    first, second = dk_end()
    gpk_ref[0] = first.astype(BF16)
    gpk_ref[1] = second.astype(BF16)
    stores[2].start()
    for i, (one, mine, sent, came) in enumerate(((dw_a, y, twa2, rwa2), (dw_b, z, twb2, rwb2))):
        one.wait_recv()
        came[mine] = sent[mine]
        last = came[0].astype(F32)
        for j in range(1, 8):
            last = last + came[j].astype(F32)
        gw_ref[i * 32:(i + 1) * 32, :] = last
    stores[4].start()

    for group in (
        (hp_x, hc_x, s_1, s_2, k_a1, k_b1, k_a2, k_b2, v_a1, v_b1, v_a2, v_b2,
         x_a, x_b, g_a, g_b),
        (ring_a, ring_b, dw_a, dw_b), dv_all, dk_all,
    ):
        for one in group:
            one.wait_send()

    def sent(k, carry):
        sibling(k, True).wait_send()
        return carry

    lax.fori_loop(0, NX, sent, 0)
    for store in stores:
        store.wait()


def hand_over(*refs):
    sources, results, held, sems = refs[:5], refs[5:10], refs[10:15], refs[15]
    loads = [pltpu.make_async_copy(a, b, sems.at[0, i]) for i, (a, b) in enumerate(zip(sources, held))]
    stores = [pltpu.make_async_copy(a, b, sems.at[1, i]) for i, (a, b) in enumerate(zip(held, results))]
    for load in loads:
        load.start()
    for load, store in zip(loads, stores):
        load.wait()
        store.start()
    for store in stores:
        store.wait()


def shards(
    cand_query, cand_key, shared_prefix_key, cand_hidden, prefix_hidden, value_matrix,
    out_cotangent, cand_scores, ranking, lengths,
):
    vmem = pl.BlockSpec(memory_space=pltpu.VMEM)
    smem = pl.BlockSpec(memory_space=pltpu.SMEM)

    def small(count):
        return [
            pltpu.VMEM((NZ, count, 16, HEAD), BF16),
            pltpu.VMEM((count, NZ, 16, HEAD), BF16),
            pltpu.VMEM((count, 16, HEAD), BF16),
            pltpu.VMEM((NZ, 16, HEAD), BF16),
        ]

    hbm = pl.BlockSpec(memory_space=pltpu.HBM)
    ring_buffers = [
        pltpu.VMEM((2, 8, 32, HEAD), BF16),
        pltpu.VMEM((2, 4, 32, HEAD), BF16),
        pltpu.VMEM((2, 8, 32, HEAD), BF16),
        pltpu.VMEM((4, 8, 32, HEAD), BF16),
    ]
    shapes = (
        jax.ShapeDtypeStruct((2, CAND, 512), BF16),
        jax.ShapeDtypeStruct((2, CAND, HEAD), BF16),
        jax.ShapeDtypeStruct((2, 16, HEAD), BF16),
        jax.ShapeDtypeStruct((2, 16, HEAD), BF16),
        jax.ShapeDtypeStruct((64, HEAD), F32),
    )
    results = pl.pallas_call(
        kernel,
        out_shape=shapes,
        in_specs=[hbm] * 7 + [smem, vmem, smem],
        out_specs=(hbm,) * 5,
        scratch_shapes=[
            *(pltpu.VMEM(one.shape, one.dtype) for one in shapes),
            pltpu.SemaphoreType.DMA((5,)),
            pltpu.VMEM((2, CAND, 512), BF16),
            pltpu.VMEM((2, CAND, HEAD), BF16),
            pltpu.VMEM((2, 16, HEAD), BF16),
            pltpu.VMEM((4, WIDTH), BF16),
            pltpu.VMEM((WIDTH, HEAD), BF16),
            pltpu.VMEM((2, CAND, 512), BF16),
            pltpu.SemaphoreType.DMA((7,)),
            pltpu.VMEM((16, 1024), F32),
            pltpu.VMEM((16, 1024), BF16),
            pltpu.VMEM((NZ, 32, 256), BF16),
            pltpu.VMEM((NY, 32, 256), BF16),
            pltpu.VMEM((NZ, 32, 256), BF16),
            pltpu.VMEM((NY, 32, 256), BF16),
            pltpu.VMEM((NZ, 2, 16, HEAD), BF16),
            pltpu.VMEM((NY, 2, 16, HEAD), BF16),
            pltpu.VMEM((NT, 32, WIDTH), BF16),
            pltpu.VMEM((NT, 16, 1024), BF16),
            pltpu.VMEM((2, 32, 16, HEAD), BF16),
            pltpu.VMEM((2, 32, 16, HEAD), BF16),
            pltpu.VMEM((HEAD, PREFIX), BF16),
            pltpu.VMEM((NYH, 8, 128), F32),
            pltpu.VMEM((NZ, 8, 128), F32),
            pltpu.VMEM((1024, HEAD), BF16),
            pltpu.VMEM((1024, HEAD), BF16),
            pltpu.VMEM((PREFIX + CAND, 1024), F32),
            pltpu.VMEM((2, CAND, HEAD), BF16),
            pltpu.VMEM((PREFIX, HEAD), F32),
            pltpu.VMEM((2, CAND, HEAD), F32),
            pltpu.VMEM((PREFIX, HEAD), F32),
            pltpu.VMEM((2, CAND, HEAD), F32),
            pltpu.VMEM((8, 2, 16, HEAD), F32),
            pltpu.VMEM((2, 32, 16, HEAD), BF16),
            pltpu.VMEM((2, 32, 16, HEAD), BF16),
            *small(NYH),
            *small(NYH),
            pltpu.VMEM((NYH, 16, HEAD), BF16),
            pltpu.VMEM((NZ, 16, HEAD), BF16),
            pltpu.VMEM((NYH, 16, HEAD), BF16),
            pltpu.VMEM((NZ, 16, HEAD), BF16),
            pltpu.VMEM((2, 64, 32, HEAD), BF16),
            *ring_buffers,
            *ring_buffers,
            pltpu.VMEM((NY, 32, HEAD), BF16),
            pltpu.VMEM((NZ, 32, HEAD), BF16),
            pltpu.VMEM((NY, 32, HEAD), BF16),
            pltpu.VMEM((NZ, 32, HEAD), BF16),
            pltpu.SemaphoreType.DMA((2, NT)),
            pltpu.SemaphoreType.DMA((2, NX)),
            pltpu.SemaphoreType.DMA((2, NX)),
            pltpu.SemaphoreType.DMA((2, 2, NZ)),
            pltpu.SemaphoreType.DMA((4, 2, NZ)),
            pltpu.SemaphoreType.DMA((4, 2, NZ)),
            pltpu.SemaphoreType.DMA((4, 2, NZ)),
            pltpu.SemaphoreType.DMA((4, 2, NZ)),
            pltpu.SemaphoreType.DMA((4, 2, NZ)),
            pltpu.SemaphoreType.DMA((2, 2, NZ)),
            pltpu.SemaphoreType.DMA((2, 2, NZ)),
            pltpu.SemaphoreType.DMA((2, 2, NZ)),
        ],
        compiler_params=pltpu.CompilerParams(
            collective_id=0, has_side_effects=True, vmem_limit_bytes=64 * 1024 * 1024
        ),
    )(
        cand_query[0],
        cand_key[0],
        shared_prefix_key.reshape(2, 16, HEAD),
        cand_hidden.reshape(32, WIDTH),
        prefix_hidden[0],
        value_matrix,
        out_cotangent[0],
        cand_scores,
        ranking,
        lengths,
    )
    gq, gck, gpk, gpv, gw = pl.pallas_call(
        hand_over,
        out_shape=shapes,
        in_specs=[pl.BlockSpec(memory_space=pl.ANY)] * 5,
        out_specs=(hbm,) * 5,
        scratch_shapes=[
            *(pltpu.VMEM(one.shape, one.dtype) for one in shapes),
            pltpu.SemaphoreType.DMA((2, 5)),
        ],
        compiler_params=pltpu.CompilerParams(vmem_limit_bytes=64 * 1024 * 1024),
    )(*results)
    return (
        gq[None],
        gck[None],
        gpk.reshape(1, 32, HEAD),
        gpv.reshape(1, 32, HEAD),
        gw,
    )


def solution(mesh):
    placed = (
        P("dp", "cand", None, "tensor"),
        P("dp", "cand", None, "tensor"),
        P("dp", "cand", "tensor"),
        P("dp", "cand", "tensor", None),
        P("dp", ("cand", "tensor"), None),
        P(None, "tensor"),
        P("dp", "cand", None, "tensor"),
        P("dp", "cand"),
        P("dp", None),
        P("dp", "cand"),
    )
    return jax.shard_map(
        shards,
        mesh=mesh,
        in_specs=placed,
        out_specs=(
            P("dp", "cand", None, "tensor"),
            P("dp", "cand", None, "tensor"),
            P("dp", "cand", "tensor"),
            P("dp", "cand", "tensor"),
            P(("dp", "cand"), "tensor"),
        ),
        check_vma=False,
    )
```

profile of v0, /device:TPU:6, one launch (start us, length us, event | category | flops | bytes accessed | tf_op | source)
XLA Modules:
  0.0 68.2 jit_solution(17444087021082137436)
XLA Ops:
  0.6 65.8 %shard_map.137 = (bf16[2,128,512]{2,1,0:T(8,128)(2,1)}, bf16[2,128,128]{2,1,0:T(8,128)(2,1)}, bf16[2,16,128]{2,1,0:T(8,128)(2,1)}, bf16[2,16,128]{2,1,0:T(8,128)(2,1)}, f32[64,128]{1,0:T(8,128)}) custom-call(bf16[2,128,512]{2,1,0:T(8,128)(2,1)} %bitcast.10, bf16[2,128,128]{2,1,0:T(8,128)(2,1)} %bitcast.13, bf16[2,16,128]{2,1,0:T(8,128)(2,1)} %bitcast.15, ...), custom_call_target="tpu_custom_call" | custom-call | tf_op jit(solution)/shard_map/pallas_call | solution.py:610
  66.4 1.8 %shard_map.138 = (bf16[2,128,512]{2,1,0:T(8,128)(2,1)}, bf16[2,128,128]{2,1,0:T(8,128)(2,1)}, bf16[2,16,128]{2,1,0:T(8,128)(2,1)}, bf16[2,16,128]{2,1,0:T(8,128)(2,1)}, f32[64,128]{1,0:T(8,128)}) custom-call(bf16[2,128,512]{2,1,0:T(8,128)(2,1)} %get-tuple-element.15.refs_0_, bf16[2,128,128]{2,1,0:T(8,128)(2,1)} %get-tuple-element.16.refs_1_, ...), custom_call_target="tpu_custom_call" | custom-call | tf_op jit(solution)/shard_map/pallas_call | solution.py:692
where the time goes:
time: 68.4 us; the launch traced here: 68.2 us
  Pallas kernels  67.6 us (99%)
    pallas_call x1, Pallas kernels, shards(): pl.pallas_call(kernel, out_shape=shapes, in_specs=[hbm] * 7 + [smem, vmem...  65.8 us
    pallas_call x1, Pallas kernels, shards(): pl.pallas_call(hand_over, out_shape=shapes, in_specs=[pl.BlockSpec(memory...  1.77 us

commit v1 on v0

--- a/solution.py
+++ b/solution.py
@@ -237,8 +237,28 @@
         return a1, b1, a2, b2
 
     hp_x = Exchange(NT, tens, at_t, lambda p: own_hp, lambda s: hp_ref.at[s], sem_hp)
-    hc_x = Exchange(NX, x, at_x, lambda p: hc_ref.at[tens],
-                    lambda s: hc_ref.at[s * 2 + core], sem_hx)
+    left, right = lax.rem(x + NX - 1, NX), lax.rem(x + 1, NX)
+    across = lax.rem(x + 2, NX)
+
+    def along(sem, block, rows, to):
+        return pltpu.make_async_remote_copy(
+            src_ref=hc_ref.at[block * 2 + core, rows],
+            dst_ref=hc_ref.at[block * 2 + core, rows],
+            send_sem=sem_hx.at[0, sem],
+            recv_sem=sem_hx.at[1, sem],
+            device_id=at_x(to),
+            device_id_type=MESH,
+        )
+
+    both, upper, lower = pl.ds(0, 32), pl.ds(0, 16), pl.ds(16, 16)
+    hc_sent = (
+        along(0, x, both, right), along(1, x, both, left),
+        along(2, left, upper, right), along(3, right, lower, left),
+    )
+    hc_came = (
+        along(0, left, both, right), along(1, right, both, left),
+        along(2, across, upper, right), along(3, across, lower, left),
+    )
     s_1 = Exchange(NYH, yh, at_yh, lambda p: s1_ref.at[yh], lambda s: s1_ref.at[s], sem_s.at[0])
     s_2 = Exchange(NZ, z, at_z, lambda p: s2_ref.at[z], lambda s: s2_ref.at[s], sem_s.at[1])
     k_a1, k_b1, k_a2, k_b2 = gather(pk_ref, kall_ref, sem_k)
@@ -258,7 +278,8 @@
     k_b1.start()
     s_1.start()
     hp_x.start()
-    hc_x.start()
+    hc_sent[0].start()
+    hc_sent[1].start()
     sibling(x, True).start()
 
     k_a1.wait_recv()
@@ -320,6 +341,11 @@
     x_a.start()
     x_b.start()
 
+    for i, block in ((0, left), (1, right)):
+        hc_came[i].wait_recv()
+        hc_sent[i + 2].start()
+        sibling(block, True).start()
+
     s_2.wait_recv()
     total = s2_ref[0]
     for i in range(1, NZ):
@@ -367,20 +393,16 @@
         dvc_ref[c] += dot(prob_c.astype(BF16), cot)
         return carry
 
-    def pass_on(k, carry):
-        sender = lax.rem(x + NX - k, NX)
-        hc_x.copy(k, sender).wait_recv()
-        sibling(sender, True).start()
-        return carry
-
-    lax.fori_loop(0, 1, soft, 0)
+    lax.fori_loop(0, 1, soft, 0, unroll=True)
+    lax.fori_loop(1, 2, soft, 0, unroll=True)
     v_a1.wait_recv()
     v_a2.start()
     v_b1.wait_recv()
     v_b2.start()
-    lax.fori_loop(1, 3, soft, 0)
-    lax.fori_loop(1, NX, pass_on, 0)
-    lax.fori_loop(3, 4, soft, 0)
+    hc_came[2].wait_recv()
+    hc_came[3].wait_recv()
+    sibling(across, True).start()
+    lax.fori_loop(2, 4, soft, 0, unroll=True)
 
     def scatter(whole, ra1, rb1, ra2, rb2, ta2, tb2, sems, ny, my_y, at_group):
         a1 = Exchange(NZ, z, at_z, lambda p: whole.at[0, pl.ds(p * ny, ny)],
@@ -453,9 +475,9 @@
     ring_b = Ring(y, at_y, send_w, 1, third_b, fourth_b, joined_b, came_b, sem_r.at[1])
     dw_a = Exchange(NY, y, at_y, lambda p: twa2.at[p], lambda s: rwa2.at[s], sem_dw.at[0])
     dw_b = Exchange(NZ, z, at_z, lambda p: twb2.at[p], lambda s: rwb2.at[s], sem_dw.at[1])
-    dv_middle()
     ring_a.start()
     ring_b.start()
+    dv_middle()
 
     cv = dot(hc_ref[...].reshape(256, WIDTH), w_ref[...]).astype(BF16).reshape(8, 2, 16, HEAD)
     for c in range(2):
@@ -484,10 +506,10 @@
         p_ref[0:128, cols] = gq_t
         return carry
 
-    lax.fori_loop(0, 1, score, 0)
+    lax.fori_loop(0, 1, score, 0, unroll=True)
     ring_a.relay()
     ring_b.relay()
-    lax.fori_loop(1, 2, score, 0)
+    lax.fori_loop(1, 2, score, 0, unroll=True)
 
     first, second = dv_end()
     gpv_ref[0] = first.astype(BF16)
@@ -499,7 +521,7 @@
     g_b = Exchange(NY, y, at_y, lambda p: gb.at[y], lambda s: gb.at[s], sem_g.at[1])
     g_a.start()
     g_b.start()
-    lax.fori_loop(2, 4, score, 0)
+    lax.fori_loop(2, 4, score, 0, unroll=True)
 
     dk_all, dk_middle, dk_end = scatter(
         send_k, rka1, rkb1, rka2, rkb2, tka2, tkb2, sem_dk, NYH, yh, at_yh
@@ -549,7 +571,7 @@
     stores[4].start()
 
     for group in (
-        (hp_x, hc_x, s_1, s_2, k_a1, k_b1, k_a2, k_b2, v_a1, v_b1, v_a2, v_b2,
+        (*hc_sent, hp_x, s_1, s_2, k_a1, k_b1, k_a2, k_b2, v_a1, v_b1, v_a2, v_b2,
          x_a, x_b, g_a, g_b),
         (ring_a, ring_b, dw_a, dw_b), dv_all, dk_all,
     ):

time: 68.4 us -> 65.2 us (0.953)
  Pallas kernels: 67.6 us -> 64.4 us
    pallas_call x1, Pallas kernels: 65.8 us -> 62.6 us  [shards(): pl.pallas_call(kernel, out_shape=shapes, in_specs=[hbm] * 7 + [smem, vmem...]
where the time goes in v1:
time: 65.2 us; the launch traced here: 65 us
  Pallas kernels  64.4 us (99%)
    pallas_call x1, Pallas kernels, shards(): pl.pallas_call(kernel, out_shape=shapes, in_specs=[hbm] * 7 + [smem, vmem...  62.6 us
    pallas_call x1, Pallas kernels, shards(): pl.pallas_call(hand_over, out_shape=shapes, in_specs=[pl.BlockSpec(memory...  1.77 us

profile of v1, /device:TPU:6, one launch (start us, length us, event | category | flops | bytes accessed | tf_op | source)
XLA Modules:
  0.0 65.0 jit_solution(11748691496834877096)
XLA Ops:
  0.6 62.6 %shard_map.137 = (bf16[2,128,512]{2,1,0:T(8,128)(2,1)}, bf16[2,128,128]{2,1,0:T(8,128)(2,1)}, bf16[2,16,128]{2,1,0:T(8,128)(2,1)}, bf16[2,16,128]{2,1,0:T(8,128)(2,1)}, f32[64,128]{1,0:T(8,128)}) custom-call(bf16[2,128,512]{2,1,0:T(8,128)(2,1)} %bitcast.10, bf16[2,128,128]{2,1,0:T(8,128)(2,1)} %bitcast.13, bf16[2,16,128]{2,1,0:T(8,128)(2,1)} %bitcast.15, ...), custom_call_target="tpu_custom_call" | custom-call | tf_op jit(solution)/shard_map/pallas_call | solution.py:632
  63.2 1.8 %shard_map.138 = (bf16[2,128,512]{2,1,0:T(8,128)(2,1)}, bf16[2,128,128]{2,1,0:T(8,128)(2,1)}, bf16[2,16,128]{2,1,0:T(8,128)(2,1)}, bf16[2,16,128]{2,1,0:T(8,128)(2,1)}, f32[64,128]{1,0:T(8,128)}) custom-call(bf16[2,128,512]{2,1,0:T(8,128)(2,1)} %get-tuple-element.15.refs_0_, bf16[2,128,128]{2,1,0:T(8,128)(2,1)} %get-tuple-element.16.refs_1_, ...), custom_call_target="tpu_custom_call" | custom-call | tf_op jit(solution)/shard_map/pallas_call | solution.py:714

commit v2 on v1

--- a/solution.py
+++ b/solution.py
@@ -14,6 +14,7 @@
 CHUNK = 256
 WIDTH = 4096
 INV_ROOT = HEAD ** (-0.5)
+EXP_SCALE = INV_ROOT * 1.4426950408889634
 
 
 def dot(a, b):
@@ -371,8 +372,8 @@
         cols = pl.ds(pl.multiple_of(n * CHUNK, CHUNK), CHUNK)
         queries = qs_ref[cols, :]
         cot = cs_ref[cols, :]
-        log_p = dot_nt(kall_ref[...].reshape(PREFIX, HEAD), queries) * INV_ROOT
-        log_c = dot_nt(ck_ref[c], queries) * INV_ROOT
+        log_p = dot_nt(kall_ref[...].reshape(PREFIX, HEAD), queries)
+        log_c = dot_nt(ck_ref[c], queries)
         slot = lax.broadcasted_iota(jnp.int32, (CAND, CHUNK), 0)
         position = lax.rem(lax.broadcasted_iota(jnp.int32, (CAND, CHUNK), 1), CAND)
         allowed = (slot <= position) & (slot < ln_ref[0, c])
@@ -380,8 +381,8 @@
         top = jnp.maximum(
             jnp.max(log_p, axis=0, keepdims=True), jnp.max(log_c, axis=0, keepdims=True)
         )
-        exp_p = jnp.exp(log_p - top)
-        exp_c = jnp.exp(log_c - top)
+        exp_p = jnp.exp2((log_p - top) * EXP_SCALE)
+        exp_c = jnp.exp2((log_c - top) * EXP_SCALE)
         inverse = 1.0 / (
             jnp.sum(exp_p, axis=0, keepdims=True) + jnp.sum(exp_c, axis=0, keepdims=True)
         )

time: 65.2 us -> 65 us (level)
  no operation moved by 1% of the time
where the time goes in v2:
time: 65 us; the launch traced here: 64.9 us
  Pallas kernels  64.2 us (99%)
    pallas_call x1, Pallas kernels, shards(): pl.pallas_call(kernel, out_shape=shapes, in_specs=[hbm] * 7 + [smem, vmem...  62.5 us
    pallas_call x1, Pallas kernels, shards(): pl.pallas_call(hand_over, out_shape=shapes, in_specs=[pl.BlockSpec(memory...  1.77 us

profile of v2, /device:TPU:6, one launch (start us, length us, event | category | flops | bytes accessed | tf_op | source)
XLA Modules:
  0.0 64.9 jit_solution(2086057260746276372)
XLA Ops:
  0.6 62.5 %shard_map.137 = (bf16[2,128,512]{2,1,0:T(8,128)(2,1)}, bf16[2,128,128]{2,1,0:T(8,128)(2,1)}, bf16[2,16,128]{2,1,0:T(8,128)(2,1)}, bf16[2,16,128]{2,1,0:T(8,128)(2,1)}, f32[64,128]{1,0:T(8,128)}) custom-call(bf16[2,128,512]{2,1,0:T(8,128)(2,1)} %bitcast.10, bf16[2,128,128]{2,1,0:T(8,128)(2,1)} %bitcast.13, bf16[2,16,128]{2,1,0:T(8,128)(2,1)} %bitcast.15, ...), custom_call_target="tpu_custom_call" | custom-call | tf_op jit(solution)/shard_map/pallas_call | solution.py:633
  63.1 1.8 %shard_map.138 = (bf16[2,128,512]{2,1,0:T(8,128)(2,1)}, bf16[2,128,128]{2,1,0:T(8,128)(2,1)}, bf16[2,16,128]{2,1,0:T(8,128)(2,1)}, bf16[2,16,128]{2,1,0:T(8,128)(2,1)}, f32[64,128]{1,0:T(8,128)}) custom-call(bf16[2,128,512]{2,1,0:T(8,128)(2,1)} %get-tuple-element.15.refs_0_, bf16[2,128,128]{2,1,0:T(8,128)(2,1)} %get-tuple-element.16.refs_1_, ...), custom_call_target="tpu_custom_call" | custom-call | tf_op jit(solution)/shard_map/pallas_call | solution.py:715
